TPU v7x, 32 devices: a whole 2x2x4 slice. The times are simulated.
32 devices in a mesh: groups: 2 (over y), wid: 4 (over z), ffn: 4 (over x, core).
Axes of the slice: x: 2, y: 2, z: 4, core: 2. Of those that a mesh axis runs over, the one named last changes fastest.
Arguments:
- tokens: bfloat16 [256, 16384], P(('groups', 'ffn'), 'wid'), parts along dimension 0, may hold values from -6 to 6
- gate_blocks: bfloat16 [4, 4, 815, 128, 128], P('wid', 'ffn'), may hold values from -0.0625 to 0.0625
- gate_slots: int32 [4, 4, 815], P('wid', 'ffn'), may hold values from 0 to 1663, as said below
- gate_count: int32 [4, 4], P('wid', 'ffn'), may hold values from 416 to 815, as said below
- up_blocks: bfloat16 [4, 4, 815, 128, 128], P('wid', 'ffn'), may hold values from -0.0625 to 0.0625
- up_slots: int32 [4, 4, 815], P('wid', 'ffn'), may hold values from 0 to 1663, as said below
- up_count: int32 [4, 4], P('wid', 'ffn'), may hold values from 416 to 815, as said below
- down_blocks: bfloat16 [4, 4, 815, 128, 128], P('ffn', 'wid'), may hold values from -0.0546875 to 0.0546875
- down_slots: int32 [4, 4, 815], P('ffn', 'wid'), may hold values from 0 to 1663, as said below
- down_count: int32 [4, 4], P('ffn', 'wid'), may hold values from 416 to 815, as said below
Outputs:
- mixed: bfloat16 [256, 16384], P(('groups', 'ffn'), 'wid'), parts along dimension 0
There are 2 independent parts, one for each index of `groups`. A program takes and returns all parts, laid end to end along the dimension named above; an argument that names none is the same for every part. Nothing has to cross between parts.
Inputs may be any that keep to these rules, and one draw needn't show every extreme that they name: `gate_slots`: each tile's 815 entries are distinct block positions of that tile; only the first count entries are kept. `gate_count`: some tile keeps 815 blocks in every draw. `up_slots`: each tile's 815 entries are distinct block positions of that tile; only the first count entries are kept. `up_count`: some tile keeps 815 blocks in every draw. `down_slots`: each tile's 815 entries are distinct block positions of that tile; only the first count entries are kept. `down_count`: some tile keeps 815 blocks in every draw.
All inputs are finite; a program needn't handle non-finite values.
Results may differ from a plain program's by a relative error of at most 0.02.
Values may be sent and summed in bfloat16 or wider, within the bound.
A program may use at most 320 MiB of HBM per device.

v0:
```python
import functools

import jax
import jax.numpy as jnp
from jax import lax
from jax.experimental import pallas as pl
from jax.experimental.pallas import tpu as pltpu
from jax.sharding import PartitionSpec as P

FF = 26624
GROUP = 4
BATCH = 4
STEP = GROUP * BATCH
DEPTH = 8


def block_lists(slots, kept, in_blocks, out_blocks):
    count = slots.shape[0]
    index = jnp.arange(count, dtype=jnp.int32)
    is_kept = index < kept
    col = jnp.where(is_kept, slots % out_blocks, out_blocks)
    row = slots // out_blocks
    rank = jnp.sum(
        (col[None, :] == col[:, None]) & (index[None, :] < index[:, None]), axis=1, dtype=jnp.int32
    )
    columns = jnp.arange(out_blocks, dtype=jnp.int32)
    number = jnp.sum(col[None, :] == columns[:, None], axis=1, dtype=jnp.int32)
    groups = (number + GROUP - 1) // GROUP
    ends = jnp.sum(
        jnp.where(columns[None, :] <= columns[:, None], groups[None, :], 0), axis=1, dtype=jnp.int32
    )
    first = jnp.sum(
        jnp.where(columns[None, :] < col[:, None], groups[None, :], 0), axis=1, dtype=jnp.int32
    )
    place = jnp.where(is_kept, first * GROUP + rank, -1)
    most = (count + out_blocks * (GROUP - 1)) // GROUP
    most = -(-most // BATCH) * BATCH
    match = place[None, :] == jnp.arange(most * GROUP, dtype=jnp.int32)[:, None]
    packed = jnp.sum(
        jnp.where(match, (index * in_blocks + row + 1)[None, :], 0), axis=1, dtype=jnp.int32
    )
    order = jnp.where(packed > 0, (packed - 1) // in_blocks, 0)
    rows = jnp.where(packed > 0, (packed - 1) % in_blocks, in_blocks)
    cols = jnp.sum(
        ends[None, :] <= jnp.arange(most, dtype=jnp.int32)[:, None], axis=1, dtype=jnp.int32
    )
    cols = jnp.minimum(cols, out_blocks - 1)
    batches = (ends[-1:] + BATCH - 1) // BATCH
    return order, rows, cols, batches


def tile_kernel(matrices, *refs):
    lists = refs[: 4 * matrices]
    x_ref = refs[4 * matrices]
    blocks = refs[4 * matrices + 1 : 5 * matrices + 1]
    out_ref, pieces, total, held, sems = refs[5 * matrices + 1 :]
    in_blocks = pieces.shape[0] - 1
    out_blocks = total.shape[0]

    def start(m, step):
        order = lists[4 * m]
        slot = lax.rem(step, DEPTH)
        for i in range(STEP):
            pltpu.make_async_copy(
                blocks[m].at[order[step * STEP + i]], held.at[m, slot, i], sems.at[m, slot]
            ).start()

    for m in range(matrices):

        @pl.loop(0, jnp.minimum(lists[4 * m + 3][0], DEPTH))
        def _(step):
            start(m, step)

    for i in range(in_blocks):
        pieces[i] = x_ref[:, i * 128 : (i + 1) * 128]
    pieces[in_blocks] = jnp.zeros(pieces.shape[1:], pieces.dtype)

    for m in range(matrices):
        rows, cols = lists[4 * m + 1], lists[4 * m + 2]
        batches = lists[4 * m + 3][0]

        @pl.loop(0, out_blocks)
        def _(o):
            total[o] = jnp.zeros(total.shape[1:], total.dtype)

        @pl.loop(0, batches)
        def _(step):
            slot = lax.rem(step, DEPTH)
            pltpu.make_async_copy(
                blocks[m].at[pl.ds(0, STEP)], held.at[m, slot], sems.at[m, slot]
            ).wait()
            for u in range(BATCH):
                base = step * STEP + u * GROUP
                piece = jnp.concatenate([pieces[rows[base + i]] for i in range(GROUP)], axis=1)
                weight = held[m, slot, u * GROUP : (u + 1) * GROUP].reshape(GROUP * 128, 128)
                product = jnp.dot(piece, weight, preferred_element_type=jnp.float32)
                o = cols[step * BATCH + u]
                total[o] = total[o] + product

            @pl.when(step + DEPTH < batches)
            def _():
                start(m, step + DEPTH)

        for o in range(out_blocks):
            at = (m * out_blocks + o) * 128
            out_ref[:, at : at + 128] = total[o].astype(out_ref.dtype)


def tile_products(operand, parts, out_blocks):
    tokens, width = operand.shape
    in_blocks = width // 128
    matrices = len(parts)
    lists = []
    for blocks, slots, kept in parts:
        lists += block_lists(slots, kept, in_blocks, out_blocks)
    count = parts[0][0].shape[0]
    smem = pl.BlockSpec(memory_space=pltpu.SMEM)
    vmem = pl.BlockSpec(memory_space=pltpu.VMEM)
    return pl.pallas_call(
        functools.partial(tile_kernel, matrices),
        out_shape=jax.ShapeDtypeStruct((tokens, matrices * out_blocks * 128), jnp.bfloat16),
        in_specs=[smem] * (4 * matrices) + [vmem] + [pl.BlockSpec(memory_space=pl.ANY)] * matrices,
        out_specs=vmem,
        scratch_shapes=[
            pltpu.VMEM((in_blocks + 1, tokens, 128), jnp.bfloat16),
            pltpu.VMEM((out_blocks, tokens, 128), jnp.float32),
            pltpu.VMEM((matrices, DEPTH, STEP, 128, 128), jnp.bfloat16),
            pltpu.SemaphoreType.DMA((matrices, DEPTH)),
        ],
        compiler_params=pltpu.CompilerParams(vmem_limit_bytes=50 * 1024 * 1024),
        cost_estimate=pl.CostEstimate(
            flops=2 * tokens * 128 * 128 * count * matrices,
            bytes_accessed=2 * 128 * 128 * count * matrices,
            transcendentals=0,
        ),
    )(*lists, operand, *[blocks for blocks, _, _ in parts])


def on_device(
    tokens,
    gate_blocks,
    gate_slots,
    gate_count,
    up_blocks,
    up_slots,
    up_count,
    down_blocks,
    down_slots,
    down_count,
):
    ffn_blocks = FF // lax.axis_size("ffn") // 128
    wid_blocks = tokens.shape[1] // 128
    full_tokens = lax.all_gather(tokens, "ffn", axis=0, tiled=True)
    partial = tile_products(
        full_tokens,
        [
            (gate_blocks[0, 0], gate_slots[0, 0], gate_count[0, 0]),
            (up_blocks[0, 0], up_slots[0, 0], up_count[0, 0]),
        ],
        ffn_blocks,
    )
    sums_both = lax.psum_scatter(partial, "wid", scatter_dimension=0, tiled=True).astype(jnp.float32)
    half_width = sums_both.shape[1] // 2
    hidden_share = (jax.nn.silu(sums_both[:, :half_width]) * sums_both[:, half_width:]).astype(
        jnp.bfloat16
    )
    hidden = lax.all_gather(hidden_share, "wid", axis=0, tiled=True)
    mixed = tile_products(
        hidden, [(down_blocks[0, 0], down_slots[0, 0], down_count[0, 0])], wid_blocks
    )
    return lax.psum_scatter(mixed, "ffn", scatter_dimension=0, tiled=True)


def solution(mesh):
    return jax.shard_map(
        on_device,
        mesh=mesh,
        in_specs=(
            P(("groups", "ffn"), "wid"),
            P("wid", "ffn", None, None, None),
            P("wid", "ffn", None),
            P("wid", "ffn"),
            P("wid", "ffn", None, None, None),
            P("wid", "ffn", None),
            P("wid", "ffn"),
            P("ffn", "wid", None, None, None),
            P("ffn", "wid", None),
            P("ffn", "wid"),
        ),
        out_specs=P(("groups", "ffn"), "wid"),
        check_vma=False,
    )
```

profile of v0, /device:TPU:0, one launch (start us, length us, event | category | flops | bytes accessed | tf_op | source)
XLA Modules:
  0.0 227.9 jit_solution(2643843475340365099)
XLA Ops:
  6.5 0.0 all-gather.3.cloned.1.call-start
  6.5 0.7 all-gather.3.cloned.1.call-update
  7.3 0.0 reduce-scatter.3.cloned.1.call-start
  7.3 0.7 remainder_reduce_fusion
  8.0 0.7 compare_reduce_fusion
  9.4 0.1 convert_reduce_fusion.3
  9.5 0.1 select_reduce_fusion.6
  9.7 0.6 slice.17
  10.9 0.7 remainder_reduce_fusion.1
  11.6 0.7 compare_reduce_fusion.1
  13.0 0.1 convert_reduce_fusion.4
  13.2 0.1 select_reduce_fusion.7
  13.3 0.6 slice.16
  14.4 0.1 select_reduce_fusion.3
  14.5 0.4 convert_reduce_fusion
  15.0 0.1 select_reduce_fusion.4
  15.1 0.1 convert_reduce_fusion.6
  15.2 0.1 convert_reduce_fusion.7
  15.3 0.4 convert_reduce_fusion.1
  15.7 0.4 select_reduce_fusion
  16.2 0.4 select_reduce_fusion.1
  16.7 11.7 %all-gather.3.cloned.1.call-done.refs_8_ = bf16[128,4096]{1,0:T(8,128)(2,1)} async-done(((bf16[32,4096]{1,0:T(8,128)(2,1)}), bf16[128,4096]{1,0:T(8,128)(2,1)}) %all-gather.3.cloned.1.call-update) | async-done | bytes 1048592 | tf_op jit(solution)/shard_map/all_gather | solution.py:153
  28.4 0.0 copy-start.1
  28.4 1.2 copy-done.1
  29.6 32.5 %shard_map.100 = bf16[128,13312]{1,0:T(8,128)(2,1)} custom-call(s32[976]{0:T(1024)S(1)} %get-tuple-element.14.refs_0_, s32[976]{0:T(1024)S(1)} %get-tuple-element.13.refs_1_, s32[244]{0:T(256)S(1)} %get-tuple-element.24.refs_2_, s32[1]{0:T(128)S(6)} %select_n.260.refs_3_, s32[976]{0:T(1024)S(1)} %get-tuple-element.21.refs_4_, ...), custom_call_target="tpu_custom_call" | custom-call | flops 6836715520 | bytes 53411840 | tf_op jit(solution)/shard_map/pallas_call | solution.py:119
  62.1 0.0 reduce-scatter.3.cloned.1.call-update
  62.2 0.0 copy-start.2
  62.2 0.0 all-gather.5.cloned.1.call-start
  62.2 71.4 %reduce-scatter.3.cloned.1.call-done = bf16[32,13312]{1,0:T(8,128)(2,1)} async-done(((bf16[128,13312]{1,0:T(8,128)(2,1)}), bf16[32,13312]{1,0:T(8,128)(2,1)}) %reduce-scatter.3.cloned.1.call-update) | async-done | bytes 851984 | tf_op jit(solution)/shard_map/reduce_scatter | solution.py:162
  133.6 1.3 convert_element_type.42
  134.8 1.0 fusion.3
  135.8 0.0 all-gather.5.cloned.1.call-update
  135.9 0.0 reduce-scatter.5.cloned.1.call-start
  136.6 0.0 copy-done.2
  136.6 0.1 convert_reduce_fusion.5
  136.7 0.1 select_reduce_fusion.8
  136.9 0.6 slice.15
  138.1 0.1 convert_reduce_fusion.8
  138.2 0.1 select_reduce_fusion.5
  138.3 0.4 convert_reduce_fusion.2
  138.7 0.4 select_reduce_fusion.2
  139.2 36.3 %all-gather.5.cloned.1.call-done.refs_4_ = bf16[128,6656]{1,0:T(8,128)(2,1)} async-done(((bf16[32,6656]{1,0:T(8,128)(2,1)}), bf16[128,6656]{1,0:T(8,128)(2,1)}) %all-gather.5.cloned.1.call-update) | async-done | bytes 1703952 | tf_op jit(solution)/shard_map/all_gather | solution.py:167
  175.5 0.0 copy-start
  175.5 1.5 copy-done
  176.9 13.5 %shard_map.101 = bf16[128,4096]{1,0:T(8,128)(2,1)} custom-call(s32[912]{0:T(1024)S(1)} %get-tuple-element.18.refs_0_, s32[912]{0:T(1024)S(1)} %get-tuple-element.17.refs_1_, s32[228]{0:T(256)S(1)} %broadcast_minimum_fusion.2.refs_2_, s32[1]{0:T(128)S(6)} %select_n.247.refs_3_, bf16[128,6656]{1,0:T(8,128)(2,1)S(1)} %copy-done, bf16[815,128,128]{2,1,0:T(8,128)(2,1)} %bitcast.14), custom_call_target="tpu_custom_call" | custom-call | flops 3418357760 | bytes 26705920 | tf_op jit(solution)/shard_map/pallas_call | solution.py:119
  190.4 0.0 reduce-scatter.5.cloned.1.call-update
  190.4 31.0 %reduce-scatter.5.cloned.1.call-done = bf16[32,4096]{1,0:T(8,128)(2,1)} async-done(((bf16[128,4096]{1,0:T(8,128)(2,1)}), bf16[32,4096]{1,0:T(8,128)(2,1)}) %reduce-scatter.5.cloned.1.call-update) | async-done | bytes 262160 | tf_op jit(solution)/shard_map/reduce_scatter | solution.py:171
  (14 shorter events, 0.1 us)
Async XLA Ops:
  6.5 21.9 %all-gather.3.cloned.1.call-start = ((), (), s32[]{:S(2)}) async-start(), calls=%async_computation.2 | async-start | bytes 1310720 | tf_op jit(solution)/shard_map/all_gather | solution.py:153
  7.3 126.3 %reduce-scatter.3.cloned.1.call-start = ((), (), s32[]{:S(2)}) async-start(), calls=%async_computation.3 | async-start | bytes 4259840 | tf_op jit(solution)/shard_map/reduce_scatter | solution.py:162
  28.4 1.2 copy-start.1
  62.2 74.4 %copy-start.2 = (s32[1,1,815]{2,1,0:T(1,128)S(1)}, s32[1,1,815]{2,1,0:T(1,128)}, u32[]{:S(2)}) copy-start(s32[1,1,815]{2,1,0:T(1,128)} %param.18) | copy-start | bytes 9784
  62.2 113.3 %all-gather.5.cloned.1.call-start = ((), (), s32[]{:S(2)}) async-start(), calls=%async_computation.4 | async-start | bytes 2129920 | tf_op jit(solution)/shard_map/all_gather | solution.py:167
  135.9 85.5 %reduce-scatter.5.cloned.1.call-start = ((), (), s32[]{:S(2)}) async-start(), calls=%async_computation.5 | async-start | bytes 1310720 | tf_op jit(solution)/shard_map/reduce_scatter | solution.py:171
  175.5 1.5 copy-start
Sparse Core Ops, SparseCore 0:
  8.9 19.4 all-gather.2
  62.3 71.2 reduce-scatter.2
  136.0 39.4 all-gather.4
  190.5 30.8 reduce-scatter.4
where the time goes:
time: 228 us
  waiting for transfers between devices  151 us (66%)
  Pallas kernels  46 us (20%)
  between operations  17.1 us (8%)
  other arithmetic  9.08 us (4%)
  local copies, waits for them, and re-layouts  4.47 us (2%)
    reduce_scatter x1, waiting for transfers between devices, on_device(): lax.psum_scatter(partial, 'wid', scatter_dimension=0, tiled=True)  71.4 us
    pallas_call x2, Pallas kernels, tile_products(): pl.pallas_call(functools.partial(tile_kernel, matrices), out_shape=jax.Sh...  46 us
    all_gather x1, waiting for transfers between devices, on_device(): hidden = lax.all_gather(hidden_share, 'wid', axis=0, tiled=True)  36.3 us
    reduce_scatter x1, waiting for transfers between devices, on_device(): return lax.psum_scatter(mixed, 'ffn', scatter_dimension=0, tiled=True)  31 us
    all_gather x1, waiting for transfers between devices, on_device(): full_tokens = lax.all_gather(tokens, 'ffn', axis=0, tiled=True)  11.7 us
  transfers between devices with their start and end apart: 4, of which 4 were waited for; matrix products, arithmetic and copies ran while one was open for 4% of the time, Pallas kernels for 0%

commit v1 on v0

--- a/solution.py
+++ b/solution.py
@@ -72,7 +72,8 @@
             start(m, step)
 
     for i in range(in_blocks):
-        pieces[i] = x_ref[:, i * 128 : (i + 1) * 128]
+        per = x_ref.shape[2] // 128
+        pieces[i] = x_ref[i // per, :, i % per * 128 : (i % per + 1) * 128]
     pieces[in_blocks] = jnp.zeros(pieces.shape[1:], pieces.dtype)
 
     for m in range(matrices):
@@ -102,13 +103,14 @@
                 start(m, step + DEPTH)
 
         for o in range(out_blocks):
-            at = (m * out_blocks + o) * 128
-            out_ref[:, at : at + 128] = total[o].astype(out_ref.dtype)
-
-
-def tile_products(operand, parts, out_blocks):
-    tokens, width = operand.shape
-    in_blocks = width // 128
+            per = out_ref.shape[3] // 128
+            at = o % per * 128
+            out_ref[o // per, m, :, at : at + 128] = total[o].astype(out_ref.dtype)
+
+
+def tile_products(operand, parts, out_blocks, chunks):
+    tokens = operand.shape[1]
+    in_blocks = operand.shape[0] * operand.shape[2] // 128
     matrices = len(parts)
     lists = []
     for blocks, slots, kept in parts:
@@ -118,7 +120,9 @@
     vmem = pl.BlockSpec(memory_space=pltpu.VMEM)
     return pl.pallas_call(
         functools.partial(tile_kernel, matrices),
-        out_shape=jax.ShapeDtypeStruct((tokens, matrices * out_blocks * 128), jnp.bfloat16),
+        out_shape=jax.ShapeDtypeStruct(
+            (chunks, matrices, tokens, out_blocks * 128 // chunks), jnp.bfloat16
+        ),
         in_specs=[smem] * (4 * matrices) + [vmem] + [pl.BlockSpec(memory_space=pl.ANY)] * matrices,
         out_specs=vmem,
         scratch_shapes=[
@@ -134,6 +138,205 @@
             transcendentals=0,
         ),
     )(*lists, operand, *[blocks for blocks, _, _ in parts])
+
+
+def hidden_kernel(n, part_ref, hid_ref, sums, send_sem, recv_sem, back_sem, home_sem):
+    me = lax.axis_index("wid")
+    chunks, _, tokens, _ = part_ref.shape
+    half = tokens // 2
+    lag = min(n, chunks)
+
+    barrier = pltpu.get_barrier_semaphore()
+    for exists, other in ((me > 0, me - 1), (me < n - 1, me + 1)):
+
+        @pl.when(exists)
+        def _():
+            pl.semaphore_signal(
+                barrier, inc=1, device_id={"wid": other}, device_id_type=pl.DeviceIdType.MESH
+            )
+
+    pl.semaphore_wait(barrier, jnp.minimum(me, 1) + jnp.minimum(n - 1 - me, 1))
+
+    def own(d, c):
+        return part_ref.at[c, :, pl.ds(d * half, half)]
+
+    def sum_copy(d, c, src):
+        return pltpu.make_async_remote_copy(
+            src_ref=src,
+            dst_ref=sums.at[d, c],
+            send_sem=send_sem.at[d, c],
+            recv_sem=recv_sem.at[d, c],
+            device_id={"wid": me + 1 if d == 0 else me - 1},
+            device_id_type=pl.DeviceIdType.MESH,
+        )
+
+    def hidden_copy(d, c):
+        rows = hid_ref.at[c, pl.ds(d * half, half)]
+        return pltpu.make_async_remote_copy(
+            src_ref=rows,
+            dst_ref=rows,
+            send_sem=back_sem.at[d, c],
+            recv_sem=home_sem.at[d, c],
+            device_id={"wid": me - 1 if d == 0 else me + 1},
+            device_id_type=pl.DeviceIdType.MESH,
+        )
+
+    def summed(d, c, m):
+        mine = part_ref[c, m, d * half : (d + 1) * half].astype(jnp.float32)
+        return sums[d, c, m].astype(jnp.float32) + mine
+
+    def reduce_chunk(d, c):
+        place = me if d == 0 else n - 1 - me
+
+        @pl.when(place == 0)
+        def _():
+            sum_copy(d, c, own(d, c)).start()
+
+        @pl.when((place > 0) & (place < n - 1))
+        def _():
+            sum_copy(d, c, sums.at[d, c]).wait_recv()
+            for m in range(2):
+                sums[d, c, m] = summed(d, c, m).astype(sums.dtype)
+            sum_copy(d, c, sums.at[d, c]).start()
+
+        @pl.when(place == n - 1)
+        def _():
+            sum_copy(d, c, sums.at[d, c]).wait_recv()
+            gate, up = summed(d, c, 0), summed(d, c, 1)
+            hid_ref[c, d * half : (d + 1) * half] = (jax.nn.silu(gate) * up).astype(hid_ref.dtype)
+            hidden_copy(d, c).start()
+
+    def spread_chunk(d, c):
+        place = me if d == 0 else n - 1 - me
+
+        @pl.when((place > 0) & (place < n - 1))
+        def _():
+            hidden_copy(d, c).wait_recv()
+            hidden_copy(d, c).start()
+
+    def finish_chunk(d, c):
+        place = me if d == 0 else n - 1 - me
+
+        @pl.when(place == 0)
+        def _():
+            hidden_copy(d, c).wait_recv()
+
+        @pl.when(place < n - 1)
+        def _():
+            sum_copy(d, c, sums.at[d, c]).wait_send()
+
+        @pl.when(place > 0)
+        def _():
+            hidden_copy(d, c).wait_send()
+
+    @pl.loop(0, chunks)
+    def _(c):
+        reduce_chunk(0, c)
+        reduce_chunk(1, c)
+
+        @pl.when(c >= lag)
+        def _():
+            spread_chunk(0, c - lag)
+            spread_chunk(1, c - lag)
+
+    @pl.loop(chunks - lag, chunks)
+    def _(c):
+        spread_chunk(0, c)
+        spread_chunk(1, c)
+
+    @pl.loop(0, chunks)
+    def _(c):
+        finish_chunk(0, c)
+        finish_chunk(1, c)
+
+
+def hidden_of(partial):
+    n = lax.axis_size("wid")
+    chunks, _, tokens, width = partial.shape
+    return pl.pallas_call(
+        functools.partial(hidden_kernel, n),
+        out_shape=jax.ShapeDtypeStruct((chunks, tokens, width), jnp.bfloat16),
+        in_specs=[pl.BlockSpec(memory_space=pltpu.VMEM)],
+        out_specs=pl.BlockSpec(memory_space=pltpu.VMEM),
+        scratch_shapes=[pltpu.VMEM((2, chunks, 2, tokens // 2, width), jnp.bfloat16)]
+        + [pltpu.SemaphoreType.DMA((2, chunks))] * 4,
+        compiler_params=pltpu.CompilerParams(
+            collective_id=0, has_side_effects=True, vmem_limit_bytes=32 * 1024 * 1024
+        ),
+    )(partial)
+
+
+def output_kernel(n, part_ref, out_ref, paired, arrived, send_1, recv_1, send_2, recv_2):
+    me = lax.axis_index("ffn")
+    core = lax.rem(me, 2)
+    chip = me // 2
+    chips = n // 2
+    sibling = me + 1 - 2 * core
+    others = [lax.rem(chip + 1 + i, chips) for i in range(chips - 1)]
+
+    barrier = pltpu.get_barrier_semaphore()
+    for device in [sibling] + [2 * k + core for k in others]:
+        pl.semaphore_signal(
+            barrier, inc=1, device_id={"ffn": device}, device_id_type=pl.DeviceIdType.MESH
+        )
+    pl.semaphore_wait(barrier, chips)
+
+    first = []
+    for i, k in enumerate(others + [chip]):
+        copy = pltpu.make_async_remote_copy(
+            src_ref=part_ref.at[2 * k + 1 - core],
+            dst_ref=paired.at[i],
+            send_sem=send_1.at[i],
+            recv_sem=recv_1.at[i],
+            device_id={"ffn": sibling},
+            device_id_type=pl.DeviceIdType.MESH,
+        )
+        copy.start()
+        first.append(copy)
+    second = []
+    for i, k in enumerate(others):
+        first[i].wait_recv()
+        mine = part_ref[2 * k + core].astype(jnp.float32)
+        paired[i] = (paired[i].astype(jnp.float32) + mine).astype(paired.dtype)
+        copy = pltpu.make_async_remote_copy(
+            src_ref=paired.at[i],
+            dst_ref=arrived.at[i],
+            send_sem=send_2.at[i],
+            recv_sem=recv_2.at[i],
+            device_id={"ffn": 2 * k + core},
+            device_id_type=pl.DeviceIdType.MESH,
+        )
+        copy.start()
+        second.append(copy)
+    first[-1].wait_recv()
+    total = part_ref[me].astype(jnp.float32) + paired[chips - 1].astype(jnp.float32)
+    for i, copy in enumerate(second):
+        copy.wait_recv()
+        total = total + arrived[i].astype(jnp.float32)
+    out_ref[...] = total.astype(out_ref.dtype)
+    for copy in first + second:
+        copy.wait_send()
+
+
+def output_of(partial):
+    n = lax.axis_size("ffn")
+    tokens, width = partial.shape
+    chips = n // 2
+    share = (tokens // n, width)
+    return pl.pallas_call(
+        functools.partial(output_kernel, n),
+        out_shape=jax.ShapeDtypeStruct(share, jnp.bfloat16),
+        in_specs=[pl.BlockSpec(memory_space=pltpu.VMEM)],
+        out_specs=pl.BlockSpec(memory_space=pltpu.VMEM),
+        scratch_shapes=[
+            pltpu.VMEM((chips,) + share, jnp.bfloat16),
+            pltpu.VMEM((chips,) + share, jnp.bfloat16),
+        ]
+        + [pltpu.SemaphoreType.DMA((chips,))] * 4,
+        compiler_params=pltpu.CompilerParams(
+            collective_id=1, has_side_effects=True, vmem_limit_bytes=32 * 1024 * 1024
+        ),
+    )(partial.reshape((n,) + share))
 
 
 def on_device(
@@ -150,25 +353,22 @@
 ):
     ffn_blocks = FF // lax.axis_size("ffn") // 128
     wid_blocks = tokens.shape[1] // 128
+    chunks = max(c for c in range(1, 17) if ffn_blocks % c == 0)
     full_tokens = lax.all_gather(tokens, "ffn", axis=0, tiled=True)
     partial = tile_products(
-        full_tokens,
+        full_tokens[None],
         [
             (gate_blocks[0, 0], gate_slots[0, 0], gate_count[0, 0]),
             (up_blocks[0, 0], up_slots[0, 0], up_count[0, 0]),
         ],
         ffn_blocks,
-    )
-    sums_both = lax.psum_scatter(partial, "wid", scatter_dimension=0, tiled=True).astype(jnp.float32)
-    half_width = sums_both.shape[1] // 2
-    hidden_share = (jax.nn.silu(sums_both[:, :half_width]) * sums_both[:, half_width:]).astype(
-        jnp.bfloat16
-    )
-    hidden = lax.all_gather(hidden_share, "wid", axis=0, tiled=True)
+        chunks,
+    )
+    hidden = hidden_of(partial)
     mixed = tile_products(
-        hidden, [(down_blocks[0, 0], down_slots[0, 0], down_count[0, 0])], wid_blocks
-    )
-    return lax.psum_scatter(mixed, "ffn", scatter_dimension=0, tiled=True)
+        hidden, [(down_blocks[0, 0], down_slots[0, 0], down_count[0, 0])], wid_blocks, 1
+    )
+    return output_of(mixed[0, 0])
 
 
 def solution(mesh):

time: 228 us -> 474 us (2.08)
  Pallas kernels: 46 us -> 433 us
  waiting for transfers between devices: 151 us -> 8.47 us
    pallas_call x0 -> x2, Pallas kernels: none -> 377 us  [the longest x1 368 us: hidden_of(): pl.pallas_call(functools.partial(hidden_kernel, n), out_shape=jax.ShapeDt...]
    reduce_scatter x2 -> x0, waiting for transfers between devices: 102 us -> none  [the longest x1 71.4 us: on_device(): lax.psum_scatter(partial, 'wid', scatter_dimension=0, tiled=True)]
    all_gather x1 -> x0, waiting for transfers between devices: 36.3 us -> none  [on_device(): hidden = lax.all_gather(hidden_share, 'wid', axis=0, tiled=True)]
    pallas_call x2, Pallas kernels: 46 us -> 56.1 us  [tile_products(): pl.pallas_call(functools.partial(tile_kernel, matrices), out_shape=jax.Sh...]
  transfers between devices with their start and end apart: 4 -> 1, of which waited for: 4 -> 1; matrix products, arithmetic and copies ran while one was open for 4% -> 2% of each run, Pallas kernels for 0% -> 0%
where the time goes in v1:
time: 474 us; the launch traced here: 472 us
  Pallas kernels  433 us (91%)
  between operations  17.5 us (4%)
  waiting for transfers between devices  8.47 us (2%)
  other arithmetic  7.49 us (2%)
  local copies, waits for them, and re-layouts  5.69 us (1%)
    pallas_call x1, Pallas kernels, hidden_of(): pl.pallas_call(functools.partial(hidden_kernel, n), out_shape=jax.ShapeDt...  368 us
    pallas_call x2, Pallas kernels, tile_products(): pl.pallas_call(functools.partial(tile_kernel, matrices), out_shape=jax.Sh...  56.1 us
  transfers between devices with their start and end apart: 1, of which 1 were waited for; matrix products, arithmetic and copies ran while one was open for 2% of the time, Pallas kernels for 0%

profile of v1, /device:TPU:0, one launch (start us, length us, event | category | flops | bytes accessed | tf_op | source)
XLA Modules:
  0.0 472.0 jit_solution(4482092823379791172)
XLA Ops:
  6.5 0.0 all-gather.2.cloned.1.call-start
  6.5 0.7 all-gather.2.cloned.1.call-update
  7.3 0.7 remainder_reduce_fusion
  8.0 0.7 compare_reduce_fusion
  9.4 0.1 convert_reduce_fusion.3
  9.5 0.1 select_reduce_fusion.6
  9.6 0.6 slice.11
  10.9 0.7 remainder_reduce_fusion.1
  11.6 0.7 compare_reduce_fusion.1
  13.0 0.1 convert_reduce_fusion.4
  13.1 0.1 select_reduce_fusion.7
  13.2 0.6 slice.10
  14.5 0.1 select_reduce_fusion.3
  14.6 0.4 convert_reduce_fusion
  15.0 0.1 select_reduce_fusion.4
  15.1 0.4 convert_reduce_fusion.1
  15.5 0.1 convert_reduce_fusion.6
  15.6 0.1 convert_reduce_fusion.7
  16.3 0.7 reduce
  17.1 0.1 convert_reduce_fusion.5
  17.2 0.1 select_reduce_fusion.8
  17.3 0.6 slice.9
  18.6 0.1 select_reduce_fusion.5
  18.7 0.4 convert_reduce_fusion.2
  19.2 0.4 select_reduce_fusion.2
  19.6 0.1 convert_reduce_fusion.8
  19.7 0.4 select_reduce_fusion
  20.2 0.4 select_reduce_fusion.1
  20.7 7.8 %all-gather.2.cloned.1.call-done = bf16[128,4096]{1,0:T(8,128)(2,1)} async-done(((bf16[32,4096]{1,0:T(8,128)(2,1)}), bf16[128,4096]{1,0:T(8,128)(2,1)}) %all-gather.2.cloned.1.call-update) | async-done | bytes 1048592 | tf_op jit(solution)/shard_map/all_gather | solution.py:357
  28.4 0.0 copy-start.1
  28.4 1.2 copy-done.1
  29.6 39.0 %shard_map.100.part_ref = bf16[13,2,128,512]{3,2,1,0:T(8,128)(2,1)} custom-call(s32[976]{0:T(1024)S(1)} %get-tuple-element.14.refs_0_, s32[976]{0:T(1024)S(1)} %get-tuple-element.13.refs_1_, s32[244]{0:T(256)S(1)} %get-tuple-element.24.refs_2_, s32[1]{0:T(128)S(6)} %select_n.260.refs_3_, s32[976]{0:T(1024)S(1)} %get-tuple-element.21.refs_4_, ...), custom_call_target="tpu_custom_call" | custom-call | flops 6836715520 | bytes 53411840 | tf_op jit(solution)/shard_map/pallas_call | solution.py:121
  68.7 0.0 copy-start
  68.7 2.0 copy-done
  70.6 368.1 %shard_map.101.refs_4_ = bf16[13,128,512]{2,1,0:T(8,128)(2,1)S(1)} custom-call(bf16[13,2,128,512]{3,2,1,0:T(8,128)(2,1)S(1)} %copy-done), custom_call_target="tpu_custom_call" | custom-call | tf_op jit(solution)/shard_map/pallas_call | solution.py:256
  438.7 17.1 %shard_map.102 = bf16[1,1,128,4096]{3,2,1,0:T(8,128)(2,1)S(1)} custom-call(s32[912]{0:T(1024)S(1)} %get-tuple-element.18.refs_0_, s32[912]{0:T(1024)S(1)} %get-tuple-element.17.refs_1_, s32[228]{0:T(256)S(1)} %broadcast_minimum_fusion.2.refs_2_, s32[1]{0:T(128)S(6)} %select_n.247.refs_3_, bf16[13,128,512]{2,1,0:T(8,128)(2,1)S(1)} %shard_map.101.refs_4_, ...), custom_call_target="tpu_custom_call" | custom-call | flops 3418357760 | bytes 26705920 | tf_op jit(solution)/shard_map/pallas_call | solution.py:121
  455.8 8.6 %shard_map.103 = bf16[32,4096]{1,0:T(8,128)(2,1)S(1)} custom-call(bf16[4,32,4096]{2,1,0:T(8,128)(2,1)S(1)} %bitcast.14), custom_call_target="tpu_custom_call" | custom-call | tf_op jit(solution)/shard_map/pallas_call | solution.py:326
  464.4 0.7 copy.15
  (13 shorter events, 0.1 us)
Async XLA Ops:
  6.5 21.9 %all-gather.2.cloned.1.call-start = ((), (), s32[]{:S(2)}) async-start(), calls=%async_computation | async-start | bytes 1310720 | tf_op jit(solution)/shard_map/all_gather | solution.py:357
  28.4 1.2 copy-start.1
  68.7 2.0 copy-start
Sparse Core Ops, SparseCore 0:
  8.9 19.4 all-gather.1

commit v2 on v1

--- a/solution.py
+++ b/solution.py
@@ -12,6 +12,8 @@
 BATCH = 4
 STEP = GROUP * BATCH
 DEPTH = 8
+SUM_LAG = 2
+BACK_LAG = 2
 
 
 def block_lists(slots, kept, in_blocks, out_blocks):
@@ -144,7 +146,6 @@
     me = lax.axis_index("wid")
     chunks, _, tokens, _ = part_ref.shape
     half = tokens // 2
-    lag = min(n, chunks)
 
     barrier = pltpu.get_barrier_semaphore()
     for exists, other in ((me > 0, me - 1), (me < n - 1, me + 1)):
@@ -185,12 +186,15 @@
         mine = part_ref[c, m, d * half : (d + 1) * half].astype(jnp.float32)
         return sums[d, c, m].astype(jnp.float32) + mine
 
+    def first_chunk(d, c):
+        place = me if d == 0 else n - 1 - me
+
+        @pl.when(place == 0)
+        def _():
+            sum_copy(d, c, own(d, c)).start()
+
     def reduce_chunk(d, c):
         place = me if d == 0 else n - 1 - me
-
-        @pl.when(place == 0)
-        def _():
-            sum_copy(d, c, own(d, c)).start()
 
         @pl.when((place > 0) & (place < n - 1))
         def _():
@@ -229,20 +233,18 @@
         def _():
             hidden_copy(d, c).wait_send()
 
-    @pl.loop(0, chunks)
-    def _(c):
-        reduce_chunk(0, c)
-        reduce_chunk(1, c)
-
-        @pl.when(c >= lag)
-        def _():
-            spread_chunk(0, c - lag)
-            spread_chunk(1, c - lag)
-
-    @pl.loop(chunks - lag, chunks)
-    def _(c):
-        spread_chunk(0, c)
-        spread_chunk(1, c)
+    def at(chunk, work, d):
+        @pl.when((chunk >= 0) & (chunk < chunks))
+        def _():
+            work(d, chunk)
+
+    @pl.loop(0, chunks + (n - 1) * (SUM_LAG + BACK_LAG))
+    def _(step):
+        for d in range(2):
+            place = me if d == 0 else n - 1 - me
+            at(step, first_chunk, d)
+            at(step - place * SUM_LAG, reduce_chunk, d)
+            at(step - (n - 1) * SUM_LAG - (n - 1 - place) * BACK_LAG, spread_chunk, d)
 
     @pl.loop(0, chunks)
     def _(c):

time: 474 us -> 176 us (0.37)
  Pallas kernels: 433 us -> 137 us
    pallas_call x1, Pallas kernels: 368 us -> 69.8 us  [hidden_of(): pl.pallas_call(functools.partial(hidden_kernel, n), out_shape=jax.ShapeDt...]
    pallas_call x1, Pallas kernels: 8.59 us -> 14.6 us  [output_of(): pl.pallas_call(functools.partial(output_kernel, n), out_shape=jax.ShapeDt...]
  transfers between devices with their start and end apart: 1 -> 1, of which waited for: 1 -> 1; matrix products, arithmetic and copies ran while one was open for 2% -> 5% of each run, Pallas kernels for 0% -> 0%
where the time goes in v2:
time: 176 us
  Pallas kernels  137 us (78%)
  between operations  17.5 us (10%)
  waiting for transfers between devices  8.47 us (5%)
  other arithmetic  7.49 us (4%)
  local copies, waits for them, and re-layouts  5.69 us (3%)
    pallas_call x1, Pallas kernels, hidden_of(): pl.pallas_call(functools.partial(hidden_kernel, n), out_shape=jax.ShapeDt...  69.8 us
    pallas_call x2, Pallas kernels, tile_products(): pl.pallas_call(functools.partial(tile_kernel, matrices), out_shape=jax.Sh...  52.2 us
    pallas_call x1, Pallas kernels, output_of(): pl.pallas_call(functools.partial(output_kernel, n), out_shape=jax.ShapeDt...  14.6 us
    all_gather x1, waiting for transfers between devices, on_device(): full_tokens = lax.all_gather(tokens, 'ffn', axis=0, tiled=True)  7.75 us
    unnamed x5, local copies, waits for them, and re-layouts  3.89 us
  transfers between devices with their start and end apart: 1, of which 1 were waited for; matrix products, arithmetic and copies ran while one was open for 5% of the time, Pallas kernels for 0%

profile of v2, /device:TPU:0, one launch (start us, length us, event | category | flops | bytes accessed | tf_op | source)
XLA Modules:
  0.0 175.8 jit_solution(8367189980787909312)
XLA Ops:
  6.5 0.0 all-gather.2.cloned.1.call-start
  6.5 0.7 all-gather.2.cloned.1.call-update
  7.3 0.7 remainder_reduce_fusion
  8.0 0.7 compare_reduce_fusion
  9.4 0.1 convert_reduce_fusion.3
  9.5 0.1 select_reduce_fusion.6
  9.6 0.6 slice.11
  10.9 0.7 remainder_reduce_fusion.1
  11.6 0.7 compare_reduce_fusion.1
  13.0 0.1 convert_reduce_fusion.4
  13.1 0.1 select_reduce_fusion.7
  13.2 0.6 slice.10
  14.5 0.1 select_reduce_fusion.3
  14.6 0.4 convert_reduce_fusion
  15.0 0.1 select_reduce_fusion.4
  15.1 0.4 convert_reduce_fusion.1
  15.5 0.1 convert_reduce_fusion.6
  15.6 0.1 convert_reduce_fusion.7
  16.3 0.7 reduce
  17.1 0.1 convert_reduce_fusion.5
  17.2 0.1 select_reduce_fusion.8
  17.3 0.6 slice.9
  18.6 0.1 select_reduce_fusion.5
  18.7 0.4 convert_reduce_fusion.2
  19.2 0.4 select_reduce_fusion.2
  19.6 0.1 convert_reduce_fusion.8
  19.7 0.4 select_reduce_fusion
  20.2 0.4 select_reduce_fusion.1
  20.7 7.8 %all-gather.2.cloned.1.call-done = bf16[128,4096]{1,0:T(8,128)(2,1)} async-done(((bf16[32,4096]{1,0:T(8,128)(2,1)}), bf16[128,4096]{1,0:T(8,128)(2,1)}) %all-gather.2.cloned.1.call-update) | async-done | bytes 1048592 | tf_op jit(solution)/shard_map/all_gather | solution.py:359
  28.4 0.0 copy-start.1
  28.4 1.2 copy-done.1
  29.6 35.2 %shard_map.100.part_ref = bf16[13,2,128,512]{3,2,1,0:T(8,128)(2,1)} custom-call(s32[976]{0:T(1024)S(1)} %get-tuple-element.14.refs_0_, s32[976]{0:T(1024)S(1)} %get-tuple-element.13.refs_1_, s32[244]{0:T(256)S(1)} %get-tuple-element.24.refs_2_, s32[1]{0:T(128)S(6)} %select_n.260.refs_3_, s32[976]{0:T(1024)S(1)} %get-tuple-element.21.refs_4_, ...), custom_call_target="tpu_custom_call" | custom-call | flops 6836715520 | bytes 53411840 | tf_op jit(solution)/shard_map/pallas_call | solution.py:123
  64.8 0.0 copy-start
  64.9 2.0 %copy-done = bf16[13,2,128,512]{3,2,1,0:T(8,128)(2,1)S(1)} copy-done((bf16[13,2,128,512]{3,2,1,0:T(8,128)(2,1)S(1)}, bf16[13,2,128,512]{3,2,1,0:T(8,128)(2,1)}, u32[]{:S(2)}) %copy-start) | copy-done | bytes 3407896
  66.8 69.8 %shard_map.101.refs_4_ = bf16[13,128,512]{2,1,0:T(8,128)(2,1)S(1)} custom-call(bf16[13,2,128,512]{3,2,1,0:T(8,128)(2,1)S(1)} %copy-done), custom_call_target="tpu_custom_call" | custom-call | tf_op jit(solution)/shard_map/pallas_call | solution.py:258
  136.7 17.0 %shard_map.102 = bf16[1,1,128,4096]{3,2,1,0:T(8,128)(2,1)S(1)} custom-call(s32[912]{0:T(1024)S(1)} %get-tuple-element.18.refs_0_, s32[912]{0:T(1024)S(1)} %get-tuple-element.17.refs_1_, s32[228]{0:T(256)S(1)} %broadcast_minimum_fusion.2.refs_2_, s32[1]{0:T(128)S(6)} %select_n.247.refs_3_, bf16[13,128,512]{2,1,0:T(8,128)(2,1)S(1)} %shard_map.101.refs_4_, ...), custom_call_target="tpu_custom_call" | custom-call | flops 3418357760 | bytes 26705920 | tf_op jit(solution)/shard_map/pallas_call | solution.py:123
  153.7 14.6 %shard_map.103 = bf16[32,4096]{1,0:T(8,128)(2,1)S(1)} custom-call(bf16[4,32,4096]{2,1,0:T(8,128)(2,1)S(1)} %bitcast.14), custom_call_target="tpu_custom_call" | custom-call | tf_op jit(solution)/shard_map/pallas_call | solution.py:328
  168.3 0.7 copy.15
  (13 shorter events, 0.1 us)
Async XLA Ops:
  6.5 21.9 %all-gather.2.cloned.1.call-start = ((), (), s32[]{:S(2)}) async-start(), calls=%async_computation | async-start | bytes 1310720 | tf_op jit(solution)/shard_map/all_gather | solution.py:359
  28.4 1.2 copy-start.1
  64.8 2.0 %copy-start = (bf16[13,2,128,512]{3,2,1,0:T(8,128)(2,1)S(1)}, bf16[13,2,128,512]{3,2,1,0:T(8,128)(2,1)}, u32[]{:S(2)}) copy-start(bf16[13,2,128,512]{3,2,1,0:T(8,128)(2,1)} %shard_map.100.part_ref) | copy-start | bytes 10223620
Sparse Core Ops, SparseCore 0:
  8.9 19.4 all-gather.1

commit v3 on v2

--- a/solution.py
+++ b/solution.py
@@ -9,9 +9,9 @@
 
 FF = 26624
 GROUP = 4
-BATCH = 4
+BATCH = 8
 STEP = GROUP * BATCH
-DEPTH = 8
+DEPTH = 6
 SUM_LAG = 2
 BACK_LAG = 2
 

time: 176 us -> 167 us (0.949)
  Pallas kernels: 137 us -> 127 us
    pallas_call x2, Pallas kernels: 52.2 us -> 40.3 us  [tile_products(): pl.pallas_call(functools.partial(tile_kernel, matrices), out_shape=jax.Sh...]
    pallas_call x1, Pallas kernels: 69.8 us -> 75.1 us  [hidden_of(): pl.pallas_call(functools.partial(hidden_kernel, n), out_shape=jax.ShapeDt...]
    pallas_call x1, Pallas kernels: 14.6 us -> 11.2 us  [output_of(): pl.pallas_call(functools.partial(output_kernel, n), out_shape=jax.ShapeDt...]
  transfers between devices with their start and end apart: 1 -> 1, of which waited for: 1 -> 1; matrix products, arithmetic and copies ran while one was open for 5% -> 6% of each run, Pallas kernels for 0% -> 0%
where the time goes in v3:
time: 167 us; the launch traced here: 166 us
  Pallas kernels  127 us (76%)
  between operations  17.5 us (10%)
  waiting for transfers between devices  8.46 us (5%)
  other arithmetic  7.5 us (4%)
  local copies, waits for them, and re-layouts  5.69 us (3%)
    pallas_call x1, Pallas kernels, hidden_of(): pl.pallas_call(functools.partial(hidden_kernel, n), out_shape=jax.ShapeDt...  75.1 us
    pallas_call x2, Pallas kernels, tile_products(): pl.pallas_call(functools.partial(tile_kernel, matrices), out_shape=jax.Sh...  40.3 us
    pallas_call x1, Pallas kernels, output_of(): pl.pallas_call(functools.partial(output_kernel, n), out_shape=jax.ShapeDt...  11.2 us
    all_gather x1, waiting for transfers between devices, on_device(): full_tokens = lax.all_gather(tokens, 'ffn', axis=0, tiled=True)  7.75 us
    unnamed x5, local copies, waits for them, and re-layouts  3.89 us
  transfers between devices with their start and end apart: 1, of which 1 were waited for; matrix products, arithmetic and copies ran while one was open for 6% of the time, Pallas kernels for 0%

profile of v3, /device:TPU:0, one launch (start us, length us, event | category | flops | bytes accessed | tf_op | source)
XLA Modules:
  0.0 165.7 jit_solution(6969997157688257446)
XLA Ops:
  6.5 0.0 all-gather.2.cloned.1.call-start
  6.5 0.7 all-gather.2.cloned.1.call-update
  7.3 0.7 remainder_reduce_fusion
  8.0 0.7 compare_reduce_fusion
  9.4 0.1 convert_reduce_fusion.3
  9.5 0.1 select_reduce_fusion.6
  9.6 0.6 slice.11
  10.9 0.7 remainder_reduce_fusion.1
  11.6 0.7 compare_reduce_fusion.1
  13.0 0.1 convert_reduce_fusion.4
  13.1 0.1 select_reduce_fusion.7
  13.2 0.6 slice.10
  14.5 0.1 select_reduce_fusion.3
  14.6 0.4 convert_reduce_fusion
  15.0 0.1 select_reduce_fusion.4
  15.1 0.4 convert_reduce_fusion.1
  15.5 0.1 convert_reduce_fusion.6
  15.6 0.1 convert_reduce_fusion.7
  16.3 0.7 reduce
  17.1 0.1 convert_reduce_fusion.5
  17.2 0.1 select_reduce_fusion.8
  17.3 0.6 slice.9
  18.6 0.1 select_reduce_fusion.5
  18.7 0.4 convert_reduce_fusion.2
  19.2 0.4 select_reduce_fusion.2
  19.6 0.1 convert_reduce_fusion.8
  19.7 0.4 select_reduce_fusion
  20.2 0.4 select_reduce_fusion.1
  20.7 7.7 %all-gather.2.cloned.1.call-done = bf16[128,4096]{1,0:T(8,128)(2,1)} async-done(((bf16[32,4096]{1,0:T(8,128)(2,1)}), bf16[128,4096]{1,0:T(8,128)(2,1)}) %all-gather.2.cloned.1.call-update) | async-done | bytes 1048592 | tf_op jit(solution)/shard_map/all_gather | solution.py:359
  28.4 0.0 copy-start.1
  28.4 1.2 copy-done.1
  29.6 27.9 %shard_map.100.part_ref = bf16[13,2,128,512]{3,2,1,0:T(8,128)(2,1)} custom-call(s32[992]{0:T(1024)S(1)} %get-tuple-element.14.refs_0_, s32[992]{0:T(1024)S(1)} %get-tuple-element.13.refs_1_, s32[248]{0:T(256)S(1)} %get-tuple-element.24.refs_2_, s32[1]{0:T(128)S(6)} %select_n.260.refs_3_, s32[992]{0:T(1024)S(1)} %get-tuple-element.21.refs_4_, ...), custom_call_target="tpu_custom_call" | custom-call | flops 6836715520 | bytes 53411840 | tf_op jit(solution)/shard_map/pallas_call | solution.py:123
  57.6 0.0 copy-start
  57.6 2.0 %copy-done = bf16[13,2,128,512]{3,2,1,0:T(8,128)(2,1)S(1)} copy-done((bf16[13,2,128,512]{3,2,1,0:T(8,128)(2,1)S(1)}, bf16[13,2,128,512]{3,2,1,0:T(8,128)(2,1)}, u32[]{:S(2)}) %copy-start) | copy-done | bytes 3407896
  59.5 75.1 %shard_map.101.refs_4_ = bf16[13,128,512]{2,1,0:T(8,128)(2,1)S(1)} custom-call(bf16[13,2,128,512]{3,2,1,0:T(8,128)(2,1)S(1)} %copy-done), custom_call_target="tpu_custom_call" | custom-call | tf_op jit(solution)/shard_map/pallas_call | solution.py:258
  134.6 12.4 %shard_map.102 = bf16[1,1,128,4096]{3,2,1,0:T(8,128)(2,1)S(1)} custom-call(s32[928]{0:T(1024)S(1)} %get-tuple-element.18.refs_0_, s32[928]{0:T(1024)S(1)} %get-tuple-element.17.refs_1_, s32[232]{0:T(256)S(1)} %broadcast_minimum_fusion.2.refs_2_, s32[1]{0:T(128)S(6)} %select_n.247.refs_3_, bf16[13,128,512]{2,1,0:T(8,128)(2,1)S(1)} %shard_map.101.refs_4_, ...), custom_call_target="tpu_custom_call" | custom-call | flops 3418357760 | bytes 26705920 | tf_op jit(solution)/shard_map/pallas_call | solution.py:123
  147.0 11.2 %shard_map.103 = bf16[32,4096]{1,0:T(8,128)(2,1)S(1)} custom-call(bf16[4,32,4096]{2,1,0:T(8,128)(2,1)S(1)} %bitcast.14), custom_call_target="tpu_custom_call" | custom-call | tf_op jit(solution)/shard_map/pallas_call | solution.py:328
  158.2 0.7 copy.15
  (13 shorter events, 0.1 us)
Async XLA Ops:
  6.5 21.9 %all-gather.2.cloned.1.call-start = ((), (), s32[]{:S(2)}) async-start(), calls=%async_computation | async-start | bytes 1310720 | tf_op jit(solution)/shard_map/all_gather | solution.py:359
  28.4 1.2 copy-start.1
  57.6 2.0 %copy-start = (bf16[13,2,128,512]{3,2,1,0:T(8,128)(2,1)S(1)}, bf16[13,2,128,512]{3,2,1,0:T(8,128)(2,1)}, u32[]{:S(2)}) copy-start(bf16[13,2,128,512]{3,2,1,0:T(8,128)(2,1)} %shard_map.100.part_ref) | copy-start | bytes 10223620
Sparse Core Ops, SparseCore 0:
  8.9 19.4 all-gather.1
